TPU v7x, 32 devices: a whole 2x2x4 slice. The times are simulated.
32 devices in a mesh: section: 2 (over core), seq: 4 (over y, x), tensor: 4 (over z).
Axes of the slice: x: 2, y: 2, z: 4, core: 2. Of those that a mesh axis runs over, the one named last changes fastest.
Arguments:
- queries: bfloat16 [2560, 8192], P(('section', 'seq'), 'tensor'), may hold values from -200 to 200
- neighbours: bfloat16 [10240, 8192], P(('section', 'seq', 'tensor')), may hold values from -6 to 6
- kv_weight: bfloat16 [2, 8192, 8192], P(None, None, 'tensor'), may hold values from -0.0625 to 0.0625
- out_weight: bfloat16 [8192, 8192], P('tensor'), may hold values from -0.5 to 0.5
- slot_map: int32 [40], replicated, may hold values from 0 to 39, as said below
Outputs:
- mixed: bfloat16 [2560, 8192], P(('section', 'seq', 'tensor'))
Inputs may be any that keep to these rules, and one draw needn't show every extreme that they name: `slot_map`: distinct numbers; slot s lies on encoder shard s // 5; at most 2 spans of one sequence shard map to one encoder shard, and that many do for some pair of shards.
All inputs are finite; a program needn't handle non-finite values.
Results may differ from a plain program's by a relative error of at most 0.013.
Values may be sent and summed in bfloat16 or wider, within the bound.
A program may use at most 256 MiB of HBM per device.

v0:
```python
import math

import jax
import jax.numpy as jnp
from jax import lax
from jax.sharding import PartitionSpec as P

HD = 128
SPAN = 64
PEER = 2
CH_DEV = 5
CAPC = 5
KEYS = 256


def attend(query_block, key_values):
    scores = jnp.einsum(
        "bqhd,bkhd->bhqk", query_block, key_values[:, :, 0], preferred_element_type=jnp.float32
    )
    scores = scores * (1.0 / math.sqrt(HD))
    peak = jnp.max(scores, axis=-1, keepdims=True)
    expo = jnp.exp(scores - peak)
    weights = (expo / jnp.sum(expo, axis=-1, keepdims=True)).astype(jnp.bfloat16)
    result = jnp.einsum(
        "bhqk,bkhd->bqhd", weights, key_values[:, :, 1], preferred_element_type=jnp.float32
    )
    return result.astype(jnp.bfloat16)


def on_device(queries, neighbours, kv_weight, out_weight, slot_map):
    groups = lax.axis_size(("section", "seq"))
    group_index = lax.axis_index(("section", "seq"))
    heads_local = kv_weight.shape[2] // HD
    per_peer = PEER
    spans = slot_map.shape[0]
    row_block = lax.all_gather(neighbours, "tensor", axis=0, tiled=True)
    result = jnp.einsum("rd,kde->rke", row_block, kv_weight, preferred_element_type=jnp.float32)
    projected = result.astype(jnp.bfloat16).reshape(row_block.shape[0], 2 * kv_weight.shape[2])
    slot_values = projected.reshape(CAPC, KEYS, 2, heads_local, HD)
    span_ids = jnp.arange(spans, dtype=jnp.int32)
    owner_shard = slot_map // CAPC
    slot_index = slot_map % CAPC
    seq_owner = span_ids // CH_DEV
    earlier = (seq_owner[:, None] == seq_owner[None, :]) & (
        owner_shard[:, None] == owner_shard[None, :]
    )
    earlier = earlier & (span_ids[None, :] < span_ids[:, None])
    arrival = jnp.sum(earlier.astype(jnp.int32), axis=1)
    target_ids = jnp.arange(groups, dtype=jnp.int32)[:, None, None]
    place_ids = jnp.arange(per_peer, dtype=jnp.int32)[None, :, None]
    selection = (seq_owner[None, None, :] == target_ids) & (arrival[None, None, :] == place_ids)
    selection = selection & (owner_shard[None, None, :] == group_index)
    send_slot = jnp.sum(jnp.where(selection, slot_index[None, None, :], 0), axis=-1)
    occupied = jnp.any(selection, axis=-1)
    own_shards = lax.dynamic_slice_in_dim(owner_shard, group_index * CH_DEV, CH_DEV)
    own_arrival = lax.dynamic_slice_in_dim(arrival, group_index * CH_DEV, CH_DEV)
    own_place = own_shards * per_peer + own_arrival
    query_blocks = queries.reshape(CH_DEV, SPAN, heads_local, HD)
    local_pairs = jnp.where(
        occupied[:, :, None, None, None, None], slot_values[send_slot], jnp.zeros((), jnp.bfloat16)
    )
    received = lax.all_to_all(
        local_pairs, ("section", "seq"), split_axis=0, concat_axis=0, tiled=True
    )
    key_values = received.reshape(groups * per_peer, KEYS, 2, heads_local, HD)[own_place]
    attended = attend(query_blocks, key_values)
    attended_flat = attended.reshape(CH_DEV * SPAN, heads_local * HD)
    mixed = lax.psum_scatter(
        jnp.dot(attended_flat, out_weight, preferred_element_type=jnp.float32),
        "tensor",
        scatter_dimension=0,
        tiled=True,
    )
    return mixed.astype(jnp.bfloat16)


def solution(mesh):
    placed = (
        P(("section", "seq"), "tensor"),
        P(("section", "seq", "tensor"), None),
        P(None, None, "tensor"),
        P("tensor", None),
        P(),
    )
    return jax.shard_map(
        on_device,
        mesh=mesh,
        in_specs=placed,
        out_specs=P(("section", "seq", "tensor"), None),
        check_vma=False,
    )
```

profile of v0, /device:TPU:0, one launch (start us, length us, event | category | flops | bytes accessed | tf_op | source)
XLA Modules:
  0.0 1189.8 jit_solution(308069179020642972)
XLA Ops:
  6.5 0.7 all-gather.2.cloned.1.call-update
  8.0 0.7 copy.15
  9.4 359.1 %all-gather.2.cloned.1.call-done = bf16[1280,8192]{1,0:T(8,128)(2,1)} async-done(((bf16[320,8192]{1,0:T(8,128)(2,1)}), bf16[1280,8192]{1,0:T(8,128)(2,1)}) %all-gather.2.cloned.1.call-update) | async-done | bytes 20971536 | tf_op jit(solution)/shard_map/all_gather | solution.py:36
  368.5 98.9 %fusion.3 = bf16[1280,2,2048]{2,0,1:T(8,128)(2,1)} fusion(bf16[2,8192,2048]{2,1,0:T(8,128)(2,1)} %param.7, bf16[1280,8192]{1,0:T(8,128)(2,1)} %all-gather.2.cloned.1.call-done), kind=kOutput, calls=%fused_computation.9 | convolution fusion | flops 85904588800 | bytes 98566144 | tf_op jit(solution)/shard_map/rd,kde->rke/dot_general | solution.py:37
  467.5 11.9 %copy.24 = bf16[320,8,16,128]{3,2,1,0:T(8,128)(2,1)} copy(bf16[320,8,16,128]{3,1,2,0:T(8,128)(2,1)} %bitcast.62) | data formatting | bytes 20971520
  479.4 10.7 fusion.32
  490.1 9.5 gather_fusion
  499.6 9.5 gather_fusion.1
  509.1 22.8 %copy_select_fusion = bf16[8,2,256,2,16,128]{5,4,3,2,1,0:T(8,128)(2,1)} fusion(pred[8,2]{1,0:T(8,128)(4,1)S(1)} %copy-done.2, bf16[8,2,128,2,16,128]{5,4,2,3,1,0:T(8,128)(2,1)} %bitcast.60, bf16[8,2,128,2,16,128]{5,4,2,3,1,0:T(8,128)(2,1)} %bitcast.59), kind=kLoop, calls=%fused_computation.6 | loop fusion | flops 33554432 | bytes 67108880 | tf_op jit(solution)/shard_map/jit(_where)/select_n | solution.py:59
  532.0 7.2 all-to-all-start
  539.5 362.8 %all-to-all-done = bf16[8,2,256,2,16,128]{5,4,3,2,1,0:T(8,128)(2,1)} async-done(((bf16[8,2,256,2,16,128]{5,4,3,2,1,0:T(8,128)(2,1)}), bf16[8,2,256,2,16,128]{5,4,3,2,1,0:T(8,128)(2,1)}, u32[]{:S(2)}, u32[]{:S(2)}) %all-to-all-start) | async-done | bytes 33554464 | tf_op jit(solution)/shard_map/all_to_all | solution.py:62
  902.4 24.7 %fusion.31 = (bf16[16,128,2,16,128]{4,3,2,1,0:T(8,128)(2,1)}, bf16[16,128,2,16,128]{4,3,2,1,0:T(8,128)(2,1)}) fusion(bf16[16,256,2,16,128]{4,3,2,1,0:T(8,128)(2,1)} %bitcast.4), kind=kLoop, calls=%fused_computation.52 | loop fusion | bytes 67108864 | tf_op jit(solution)/shard_map/gather | solution.py:65
  927.1 9.7 gather_fusion.2
  936.8 6.8 copy_dynamic-update-slice_fusion.1
  943.6 9.9 gather_fusion.3
  953.5 6.9 copy_dynamic-update-slice_fusion
  960.3 4.4 fusion.7
  964.8 2.4 copy-done
  967.1 1.9 fusion.33
  969.1 14.6 %fusion.16 = bf16[5,64,16,128]{3,1,2,0:T(8,128)(2,1)S(1)} fusion(bf16[5,256,2,16,128]{4,1,3,0,2:T(8,128)(2,1)} %copy_dynamic-update-slice_fusion, f32[5,16,64]{2,1,0:T(8,128)S(1)} %fusion.33, f32[5,16,256,64]{2,3,1,0:T(8,128)} %copy-done), kind=kOutput, calls=%fused_computation.25 | convolution fusion | flops 342758656 | bytes 17059840 | tf_op jit(solution)/shard_map/bhqk,bkhd->bqhd/dot_general | solution.py:24
  983.7 1.1 copy.22
  984.8 19.3 %fusion.17 = f32[320,8192]{1,0:T(8,128)} fusion(bf16[2048,8192]{1,0:T(8,128)(2,1)} %param.8, bf16[40,8,16,128]{3,2,1,0:T(8,128)(2,1)S(1)} %bitcast.65), kind=kOutput, calls=%fused_computation.26 | convolution fusion | flops 10737418240 | bytes 45350912 | tf_op jit(solution)/shard_map/dot_general | solution.py:69
  1004.1 175.5 %reduce-scatter.2.cloned.1.call-done = f32[80,8192]{1,0:T(8,128)} async-done(((f32[320,8192]{1,0:T(8,128)}), f32[80,8192]{1,0:T(8,128)}) %reduce-scatter.2.cloned.1.call-update) | async-done | bytes 2621456 | tf_op jit(solution)/shard_map/reduce_scatter | solution.py:68
  1179.6 2.9 convert_element_type.23
  (24 shorter events, 1.7 us)
Async XLA Ops:
  6.5 0.7 copy-start.3
  6.5 362.0 %all-gather.2.cloned.1.call-start = ((), (), s32[]{:S(2)}) async-start(), calls=%async_computation.2 | async-start | bytes 26214400 | tf_op jit(solution)/shard_map/all_gather | solution.py:36
  499.6 9.5 copy-start.2
  531.9 7.3 copy-start.1
  532.0 370.4 %all-to-all-start = ((bf16[8,2,256,2,16,128]{5,4,3,2,1,0:T(8,128)(2,1)}), bf16[8,2,256,2,16,128]{5,4,3,2,1,0:T(8,128)(2,1)}, u32[]{:S(2)}, u32[]{:S(2)}) async-start(bf16[8,2,256,2,16,128]{5,4,3,2,1,0:T(8,128)(2,1)} %copy_select_fusion), calls=%async_computation | async-start | bytes 67108864 | tf_op jit(solution)/shard_map/all_to_all | solution.py:62
  539.2 640.4 %reduce-scatter.2.cloned.1.call-start = ((), (), s32[]{:S(2)}) async-start(), calls=%async_computation.3 | async-start | bytes 13107200 | tf_op jit(solution)/shard_map/reduce_scatter | solution.py:68
  964.8 2.4 copy-start
Sparse Core Ops, SparseCore 0:
  8.9 359.5 all-gather.1
  1004.2 175.2 reduce-scatter.1
where the time goes:
time: 1200 us; the launch traced here: 1190 us
  waiting for transfers between devices  898 us (75%)
  matrix products  137 us (11%)
  local copies, waits for them, and re-layouts  104 us (9%)
  other arithmetic  28.9 us (2%)
  between operations  14 us (1%)
    all_to_all x1, waiting for transfers between devices, on_device(): lax.all_to_all(local_pairs, ('section', 'seq'), split_axis=0, concat_axis...  363 us
    all_gather x1, waiting for transfers between devices, on_device(): row_block = lax.all_gather(neighbours, 'tensor', axis=0, tiled=True)  359 us
    reduce_scatter x1, waiting for transfers between devices, on_device(): lax.psum_scatter(jnp.dot(attended_flat, out_weight, preferred_element_typ...  175 us
    dot_general x1, matrix products, on_device(): jnp.einsum('rd,kde->rke', row_block, kv_weight, preferred_element_type=jn...  98.9 us
    gather x3, local copies, waits for them, and re-layouts, on_device(): received.reshape(groups * per_peer, KEYS, 2, heads_local, HD)[own_place]  44.3 us
    gather x3, local copies, waits for them, and re-layouts, on_device(): slot_values[send_slot]  29.7 us
    unnamed x12, local copies, waits for them, and re-layouts  28.2 us
  transfers between devices with their start and end apart: 3, of which 3 were waited for; matrix products, arithmetic and copies ran while one was open for 0% of the time, Pallas kernels for 0%

commit v1 on v0

v1 whole, which is shorter than its diff:
```python
import math

import jax
import jax.numpy as jnp
from jax import lax
from jax.experimental import pallas as pl
from jax.experimental.pallas import tpu as pltpu
from jax.sharding import PartitionSpec as P

HD = 128
SPAN = 64
PEER = 2
CH_DEV = 5
CAPC = 5
KEYS = 256
HEADS_STEP = 4
PARTS = 2
OUTER = ("section", "seq")


def attend_kernel(q_ref, k_ref, v_ref, o_ref):
    for h in range(q_ref.shape[2] // HD):
        cols = slice(h * HD, (h + 1) * HD)
        scores = lax.dot_general(
            q_ref[0, :, cols],
            k_ref[:, cols],
            (((1,), (1,)), ((), ())),
            preferred_element_type=jnp.float32,
        ) * (1.0 / math.sqrt(HD))
        peak = jnp.max(scores, axis=-1, keepdims=True)
        expo = jnp.exp(scores - peak)
        weights = (expo / jnp.sum(expo, axis=-1, keepdims=True)).astype(jnp.bfloat16)
        o_ref[0, :, cols] = jnp.dot(
            weights, v_ref[:, cols], preferred_element_type=jnp.float32
        ).astype(o_ref.dtype)


def attend(query_blocks, key_values):
    slots, span, width = query_blocks.shape
    step = math.gcd(HEADS_STEP * HD, width)
    steps = width // step
    return pl.pallas_call(
        attend_kernel,
        grid=(slots, steps),
        in_specs=[
            pl.BlockSpec((1, span, step), lambda s, h: (s, 0, h)),
            pl.BlockSpec((KEYS, step), lambda s, h: (s, h)),
            pl.BlockSpec((KEYS, step), lambda s, h: (s, h + steps)),
        ],
        out_specs=pl.BlockSpec((1, span, step), lambda s, h: (s, 0, h)),
        out_shape=jax.ShapeDtypeStruct(query_blocks.shape, jnp.bfloat16),
        cost_estimate=pl.CostEstimate(
            flops=4 * slots * span * KEYS * width,
            bytes_accessed=4 * slots * (span + KEYS) * width,
            transcendentals=slots * span * KEYS * (width // HD),
        ),
    )(query_blocks, key_values, key_values)


def pick(array, index, count):
    return jnp.concatenate(
        [lax.dynamic_slice_in_dim(array, index[i], 1, 0) for i in range(count)], axis=0
    )


def on_device(queries, neighbours, kv_weight, out_weight, slot_map):
    groups = lax.axis_size(OUTER)
    tensors = lax.axis_size("tensor")
    group = lax.axis_index(OUTER)
    width = kv_weight.shape[2]
    spans = slot_map.shape[0]
    depth = neighbours.shape[1]

    span_ids = jnp.arange(spans, dtype=jnp.int32)
    owner_shard = slot_map // CAPC
    seq_owner = span_ids // CH_DEV
    earlier = (seq_owner[:, None] == seq_owner[None, :]) & (
        owner_shard[:, None] == owner_shard[None, :]
    )
    earlier = earlier & (span_ids[None, :] < span_ids[:, None])
    arrival = jnp.sum(earlier.astype(jnp.int32), axis=1)
    peers = jnp.arange(groups * PEER, dtype=jnp.int32)[:, None]
    out_hit = (owner_shard * PEER + arrival)[None, :] == peers
    out_hit = out_hit & (seq_owner == group)[None, :]
    ask = jnp.sum(jnp.where(out_hit, (span_ids % CH_DEV)[None, :], 0), axis=1)
    back_hit = (seq_owner * PEER + arrival)[None, :] == peers
    back_hit = back_hit & (owner_shard == group)[None, :]
    answer = jnp.sum(jnp.where(back_hit, (slot_map % CAPC)[None, :], 0), axis=1)
    slots = group * CAPC + jnp.arange(CAPC, dtype=jnp.int32)[:, None]
    asked = jnp.sum(
        jnp.where(slot_map[None, :] == slots, (seq_owner * PEER + arrival)[None, :], 0),
        axis=1,
    )
    own = group * CH_DEV + jnp.arange(CH_DEV, dtype=jnp.int32)[:, None]
    answered = jnp.sum(
        jnp.where(span_ids[None, :] == own, (owner_shard * PEER + arrival)[None, :], 0),
        axis=1,
    )

    rows_out = queries.shape[0] // tensors
    run = math.gcd(rows_out, SPAN) // PARTS
    query_rows = queries.reshape(CH_DEV, SPAN // (run * PARTS), PARTS, run, width)
    query_rows = query_rows.transpose(0, 2, 1, 3, 4).reshape(CH_DEV, SPAN, width)
    sent = pick(query_rows, ask, groups * PEER)
    got = lax.all_to_all(sent, OUTER, split_axis=0, concat_axis=0, tiled=True)
    query_blocks = pick(got, asked, CAPC)

    pieces = CAPC
    unit = neighbours.shape[0] // pieces
    key_values = jnp.zeros((tensors, pieces, unit, 2 * width), jnp.bfloat16)
    for i in range(pieces):
        block = lax.all_gather(
            neighbours[i * unit : (i + 1) * unit], "tensor", axis=0, tiled=True
        )
        part = jnp.einsum("rd,kde->rke", block, kv_weight, preferred_element_type=jnp.float32)
        part = part.astype(jnp.bfloat16).reshape(tensors, 1, unit, 2 * width)
        key_values = lax.dynamic_update_slice(key_values, part, (0, i, 0, 0))
    key_values = key_values.reshape(CAPC * KEYS, 2 * width)

    attended = attend(query_blocks, key_values)

    outs = []
    part_rows = SPAN // PARTS
    for c in range(PARTS):
        piece = attended[:, c * part_rows : (c + 1) * part_rows]
        back = lax.all_to_all(
            pick(piece, answer, groups * PEER), OUTER, split_axis=0, concat_axis=0, tiled=True
        )
        mine = pick(back, answered, CH_DEV).reshape(CH_DEV * part_rows, width)
        total = jnp.dot(mine, out_weight, preferred_element_type=jnp.float32)
        outs.append(
            lax.psum_scatter(
                total.astype(jnp.bfloat16), "tensor", scatter_dimension=0, tiled=True
            ).reshape(rows_out // (run * PARTS), 1, run, depth)
        )
    return jnp.concatenate(outs, axis=1).reshape(rows_out, depth)


def solution(mesh):
    placed = (
        P(("section", "seq"), "tensor"),
        P(("section", "seq", "tensor"), None),
        P(None, None, "tensor"),
        P("tensor", None),
        P(),
    )
    return jax.shard_map(
        on_device,
        mesh=mesh,
        in_specs=placed,
        out_specs=P(("section", "seq", "tensor"), None),
        check_vma=False,
    )
```

time: 1200 us -> 689 us (0.57)
  waiting for transfers between devices: 898 us -> 231 us
  between operations: 14 us -> 93.5 us
  matrix products: 137 us -> 168 us
  Pallas kernels: 0 us -> 30.6 us
  blocking collectives: 0 us -> 30 us
  other arithmetic: 28.9 us -> 2.06 us
    all_to_all x1 -> x2, waiting for transfers between devices: 363 us -> 16.8 us  [the longest x1 16.8 us: on_device(): lax.all_to_all(pick(piece, answer, groups * PEER), OUTER, split_axis=0, c...]
    all_gather x1 -> x5, waiting for transfers between devices: 359 us -> 154 us  [on_device(): lax.all_gather(neighbours[i * unit:(i + 1) * unit], 'tensor', axis=0, til...]
    reduce_scatter x1 -> x2, waiting for transfers between devices: 175 us -> 56.9 us  [on_device(): lax.psum_scatter(total.astype(jnp.bfloat16), 'tensor', scatter_dimension=...]
    gather x6 -> x0, local copies, waits for them, and re-layouts: 74.1 us -> none  [the longest x3 44.3 us: on_device(): received.reshape(groups * per_peer, KEYS, 2, heads_local, HD)[own_place]]
    dot_general x4 -> x7, matrix products: 137 us -> 168 us  [the longest x5 138 us: on_device(): jnp.einsum('rd,kde->rke', block, kv_weight, preferred_element_type=jnp.fl...]
    pallas_call x0 -> x1, Pallas kernels: none -> 30.6 us  [attend(): pl.pallas_call(attend_kernel, grid=(slots, steps), in_specs=[pl.BlockSpec...]
    all_to_all x0 -> x1, blocking collectives: none -> 30 us  [on_device(): lax.all_to_all(pick(piece, answer, groups * PEER), OUTER, split_axis=0, c...]
    select_n x4 -> x1, other arithmetic: 22.9 us -> 0.01 us  [on_device(): answer = jnp.sum(jnp.where(back_hit, (slot_map % CAPC)[None, :], 0), axis=1)]
  transfers between devices with their start and end apart: 3 -> 9, of which waited for: 3 -> 7; matrix products, arithmetic and copies ran while one was open for 0% -> 28% of each run, Pallas kernels for 0% -> 0%
where the time goes in v1:
time: 689 us; the launch traced here: 677 us
  waiting for transfers between devices  231 us (34%)
  matrix products  168 us (24%)
  local copies, waits for them, and re-layouts  114 us (17%)
  between operations  93.5 us (14%)
  Pallas kernels  30.6 us (4%)
  blocking collectives  30 us (4%)
  starting transfers between devices  9.1 us (1%)
    all_gather x5, waiting for transfers between devices, on_device(): lax.all_gather(neighbours[i * unit:(i + 1) * unit], 'tensor', axis=0, til...  154 us
    dot_general x5, matrix products, on_device(): jnp.einsum('rd,kde->rke', block, kv_weight, preferred_element_type=jnp.fl...  138 us
    reduce_scatter x2, waiting for transfers between devices, on_device(): lax.psum_scatter(total.astype(jnp.bfloat16), 'tensor', scatter_dimension=...  56.9 us
    unnamed x69, local copies, waits for them, and re-layouts  40.1 us
    pallas_call x1, Pallas kernels, attend(): pl.pallas_call(attend_kernel, grid=(slots, steps), in_specs=[pl.BlockSpec...  30.6 us
    dot_general x2, matrix products, on_device(): total = jnp.dot(mine, out_weight, preferred_element_type=jnp.float32)  30.2 us
    all_to_all x1, blocking collectives, on_device(): lax.all_to_all(pick(piece, answer, groups * PEER), OUTER, split_axis=0, c...  30 us
    reshape x5, local copies, waits for them, and re-layouts, on_device(): part = part.astype(jnp.bfloat16).reshape(tensors, 1, unit, 2 * width)  21.3 us
  transfers between devices with their start and end apart: 9, of which 7 were waited for; matrix products, arithmetic and copies ran while one was open for 28% of the time, Pallas kernels for 0%

profile of v1, /device:TPU:0, one launch (start us, length us, event | category | flops | bytes accessed | tf_op | source)
XLA Modules:
  0.0 677.4 jit_solution(14240604040699761397)
XLA Ops:
  6.5 4.9 fusion.28
  57.0 5.2 all-to-all-start
  122.4 27.0 %fusion.10 = bf16[256,2,2048]{2,0,1:T(8,128)(2,1)S(1)} fusion(bf16[2,8192,2048]{2,1,0:T(8,128)(2,1)} %param.7, bf16[256,8192]{1,0:T(8,128)(2,1)} %all-gather.6.cloned.1.call-done), kind=kOutput, calls=%fused_computation.12 | convolution fusion | flops 17180917760 | bytes 73400320 | tf_op jit(solution)/shard_map/rd,kde->rke/dot_general | solution.py:115
  156.2 19.8 %all-gather.8.cloned.1.call-done = bf16[256,8192]{1,0:T(8,128)(2,1)} async-done(((bf16[64,8192]{1,0:T(8,128)(2,1)}), bf16[256,8192]{1,0:T(8,128)(2,1)}) %all-gather.8.cloned.1.call-update) | async-done | bytes 4194320 | tf_op jit(solution)/shard_map/all_gather | solution.py:112
  176.0 27.8 %fusion.13 = bf16[256,2,2048]{2,0,1:T(8,128)(2,1)S(1)} fusion(bf16[2,8192,2048]{2,1,0:T(8,128)(2,1)} %param.7, bf16[256,8192]{1,0:T(8,128)(2,1)} %all-gather.8.cloned.1.call-done), kind=kOutput, calls=%fused_computation.13 | convolution fusion | flops 17180917760 | bytes 73400320 | tf_op jit(solution)/shard_map/rd,kde->rke/dot_general | solution.py:115
  207.4 4.5 reshape.94
  211.8 45.0 %all-gather.10.cloned.1.call-done = bf16[256,8192]{1,0:T(8,128)(2,1)} async-done(((bf16[64,8192]{1,0:T(8,128)(2,1)}), bf16[256,8192]{1,0:T(8,128)(2,1)}) %all-gather.10.cloned.1.call-update) | async-done | bytes 4194320 | tf_op jit(solution)/shard_map/all_gather | solution.py:112
  256.9 28.1 %fusion.16 = bf16[256,2,2048]{2,0,1:T(8,128)(2,1)S(1)} fusion(bf16[2,8192,2048]{2,1,0:T(8,128)(2,1)} %param.7, bf16[256,8192]{1,0:T(8,128)(2,1)} %all-gather.10.cloned.1.call-done), kind=kOutput, calls=%fused_computation.14 | convolution fusion | flops 17180917760 | bytes 73400320 | tf_op jit(solution)/shard_map/rd,kde->rke/dot_general | solution.py:115
  288.5 4.5 reshape.95
  293.0 44.6 %all-gather.12.cloned.1.call-done = bf16[256,8192]{1,0:T(8,128)(2,1)} async-done(((bf16[64,8192]{1,0:T(8,128)(2,1)}), bf16[256,8192]{1,0:T(8,128)(2,1)}) %all-gather.12.cloned.1.call-update) | async-done | bytes 4194320 | tf_op jit(solution)/shard_map/all_gather | solution.py:112
  337.6 27.8 %fusion.19 = bf16[256,2,2048]{2,0,1:T(8,128)(2,1)S(1)} fusion(bf16[2,8192,2048]{2,1,0:T(8,128)(2,1)} %param.7, bf16[256,8192]{1,0:T(8,128)(2,1)} %all-gather.12.cloned.1.call-done), kind=kOutput, calls=%fused_computation.15 | convolution fusion | flops 17180917760 | bytes 73400320 | tf_op jit(solution)/shard_map/rd,kde->rke/dot_general | solution.py:115
  368.9 4.5 reshape.96
  373.4 44.9 %all-gather.14.cloned.1.call-done = bf16[256,8192]{1,0:T(8,128)(2,1)} async-done(((bf16[64,8192]{1,0:T(8,128)(2,1)}), bf16[256,8192]{1,0:T(8,128)(2,1)}) %all-gather.14.cloned.1.call-update) | async-done | bytes 4194320 | tf_op jit(solution)/shard_map/all_gather | solution.py:112
  418.4 26.9 %fusion.22 = bf16[256,2,2048]{2,0,1:T(8,128)(2,1)S(1)} fusion(bf16[2,8192,2048]{2,1,0:T(8,128)(2,1)} %param.7, bf16[256,8192]{1,0:T(8,128)(2,1)} %all-gather.14.cloned.1.call-done), kind=kOutput, calls=%fused_computation.16 | convolution fusion | flops 17180917760 | bytes 73400320 | tf_op jit(solution)/shard_map/rd,kde->rke/dot_general | solution.py:115
  448.8 4.5 reshape.97
  453.3 5.3 dynamic_update_slice.15
  467.1 9.5 %copy.22 = bf16[4,5,64,4096]{3,2,1,0:T(8,128)(2,1)} copy(bf16[4,5,64,4096]{3,2,0,1:T(8,128)(2,1)} %constant_dynamic-update-slice_fusion.42) | data formatting | bytes 20971520 | tf_op jit(solution)/shard_map/dynamic_update_slice | solution.py:117
  476.6 30.6 %shard_map.55 = bf16[5,64,2048]{2,1,0:T(8,128)(2,1)} custom-call(bf16[5,64,2048]{2,1,0:T(8,128)(2,1)} %dynamic-slice_dynamic-update-slice_fusion.q_ref, bf16[1280,4096]{1,0:T(8,128)(2,1)} %bitcast.86, bf16[1280,4096]{1,0:T(8,128)(2,1)} %bitcast.87), custom_call_target="tpu_custom_call" | custom-call | flops 671088640 | bytes 13107200 | tf_op jit(solution)/shard_map/pallas_call | solution.py:42
  519.2 3.7 all-to-all-start.1
  532.2 16.8 %all-to-all-done.1 = bf16[16,32,2048]{2,1,0:T(8,128)(2,1)S(1)} async-done(((bf16[16,32,2048]{2,1,0:T(8,128)(2,1)}), bf16[16,32,2048]{2,1,0:T(8,128)(2,1)S(1)}, u32[]{:S(2)}, u32[]{:S(2)}) %all-to-all-start.1) | async-done | bytes 2097184 | tf_op jit(solution)/shard_map/all_to_all | solution.py:126
  549.1 15.0 %convolution_convert_fusion.1 = bf16[160,8192]{1,0:T(8,128)(2,1)} fusion(bf16[160,2048]{1,0:T(8,128)(2,1)S(1)} %bitcast.108, bf16[2048,8192]{1,0:T(8,128)(2,1)} %param.8), kind=kOutput, calls=%fused_computation.1 | convolution fusion | flops 5370019840 | bytes 36831232 | tf_op jit(solution)/shard_map/dot_general | solution.py:130
  565.5 30.0 %all_to_all.15 = bf16[16,32,2048]{2,1,0:T(8,128)(2,1)S(1)} all-to-all(bf16[16,32,2048]{2,1,0:T(8,128)(2,1)} %constant_dynamic-update-slice_fusion.21), channel_id=1, replica_groups=mesh['section'=2,'seq'=4,'tensor'=4] {'section','seq'}, dimensions={0} | all-to-all | bytes 4194304 | tf_op jit(solution)/shard_map/all_to_all | solution.py:126
  595.6 15.2 %convolution_convert_fusion = bf16[160,8192]{1,0:T(8,128)(2,1)} fusion(bf16[160,2048]{1,0:T(8,128)(2,1)S(1)} %bitcast.107, bf16[2048,8192]{1,0:T(8,128)(2,1)} %param.8), kind=kOutput, calls=%fused_computation | convolution fusion | flops 5370019840 | bytes 36831232 | tf_op jit(solution)/shard_map/dot_general | solution.py:130
  613.6 54.1 %reduce-scatter.5.cloned.1.call-done = bf16[40,8192]{1,0:T(8,128)(2,1)} async-done(((bf16[160,8192]{1,0:T(8,128)(2,1)}), bf16[40,8192]{1,0:T(8,128)(2,1)}) %reduce-scatter.5.cloned.1.call-update) | async-done | bytes 655376 | tf_op jit(solution)/shard_map/reduce_scatter | solution.py:132
  (119 shorter events, 83.7 us)
Async XLA Ops:
  6.5 115.9 %all-gather.6.cloned.1.call-start = ((), (), s32[]{:S(2)}) async-start(), calls=%async_computation.5 | async-start | bytes 5242880 | tf_op jit(solution)/shard_map/all_gather | solution.py:112
  11.4 2.1 copy-start.5
  11.4 5.9 copy-start.4
  11.5 164.5 %all-gather.8.cloned.1.call-start = ((), (), s32[]{:S(2)}) async-start(), calls=%async_computation.6 | async-start | bytes 5242880 | tf_op jit(solution)/shard_map/all_gather | solution.py:112
  12.2 244.7 %all-gather.10.cloned.1.call-start = ((), (), s32[]{:S(2)}) async-start(), calls=%async_computation.7 | async-start | bytes 5242880 | tf_op jit(solution)/shard_map/all_gather | solution.py:112
  12.9 324.7 %all-gather.12.cloned.1.call-start = ((), (), s32[]{:S(2)}) async-start(), calls=%async_computation.8 | async-start | bytes 5242880 | tf_op jit(solution)/shard_map/all_gather | solution.py:112
  57.0 57.0 %all-to-all-start = ((bf16[16,64,2048]{2,1,0:T(8,128)(2,1)}), bf16[16,64,2048]{2,1,0:T(8,128)(2,1)}, u32[]{:S(2)}, u32[]{:S(2)}) async-start(bf16[16,64,2048]{2,1,0:T(8,128)(2,1)} %dynamic-slice_dynamic-update-slice_fusion.5), calls=%async_computation | async-start | bytes 8388608 | tf_op jit(solution)/shard_map/all_to_all | solution.py:105
  62.2 356.2 %all-gather.14.cloned.1.call-start = ((), (), s32[]{:S(2)}) async-start(), calls=%async_computation.9 | async-start | bytes 5242880 | tf_op jit(solution)/shard_map/all_gather | solution.py:112
  453.3 5.3 copy-start
  458.6 2.3 copy-start.1
  460.9 2.3 copy-start.2
  463.3 2.3 copy-start.3
  519.2 29.8 %all-to-all-start.1 = ((bf16[16,32,2048]{2,1,0:T(8,128)(2,1)}), bf16[16,32,2048]{2,1,0:T(8,128)(2,1)S(1)}, u32[]{:S(2)}, u32[]{:S(2)}) async-start(bf16[16,32,2048]{2,1,0:T(8,128)(2,1)} %constant_dynamic-update-slice_fusion), calls=%async_computation.1 | async-start | bytes 4194304 | tf_op jit(solution)/shard_map/all_to_all | solution.py:126
  522.9 90.8 %reduce-scatter.3.cloned.1.call-start = ((), (), s32[]{:S(2)}) async-start(), calls=%async_computation.10 | async-start | bytes 3276800 | tf_op jit(solution)/shard_map/reduce_scatter | solution.py:132
  564.1 103.6 %reduce-scatter.5.cloned.1.call-start = ((), (), s32[]{:S(2)}) async-start(), calls=%async_computation.11 | async-start | bytes 3276800 | tf_op jit(solution)/shard_map/reduce_scatter | solution.py:132
Sparse Core Ops, SparseCore 0:
  11.6 83.4 all-gather.5
  96.6 79.3 all-gather.7
  177.6 79.2 all-gather.9
  258.3 79.2 all-gather.11
  339.0 79.2 all-gather.13
  564.3 49.2 reduce-scatter.2
  615.9 51.7 reduce-scatter.4

commit v2 on v1

--- a/solution.py
+++ b/solution.py
@@ -1,3 +1,4 @@
+import functools
 import math
 
 import jax
@@ -13,48 +14,78 @@
 CH_DEV = 5
 CAPC = 5
 KEYS = 256
-HEADS_STEP = 4
+HEADS_STEP = 2
+FIRST = 4
 PARTS = 2
 OUTER = ("section", "seq")
 
 
-def attend_kernel(q_ref, k_ref, v_ref, o_ref):
-    for h in range(q_ref.shape[2] // HD):
-        cols = slice(h * HD, (h + 1) * HD)
-        scores = lax.dot_general(
-            q_ref[0, :, cols],
-            k_ref[:, cols],
-            (((1,), (1,)), ((), ())),
-            preferred_element_type=jnp.float32,
-        ) * (1.0 / math.sqrt(HD))
-        peak = jnp.max(scores, axis=-1, keepdims=True)
-        expo = jnp.exp(scores - peak)
-        weights = (expo / jnp.sum(expo, axis=-1, keepdims=True)).astype(jnp.bfloat16)
-        o_ref[0, :, cols] = jnp.dot(
-            weights, v_ref[:, cols], preferred_element_type=jnp.float32
-        ).astype(o_ref.dtype)
+def attend_kernel(unit, first, rows_ref, weight_ref, before_ref, query_ref, *out_refs):
+    rows = rows_ref[...]
+    last = [
+        jnp.dot(rows, weight_ref[k], preferred_element_type=jnp.float32).astype(jnp.bfloat16)
+        for k in range(2)
+    ]
+    part_rows = SPAN // len(out_refs)
+    for s in range(CAPC):
+        key_value = []
+        for k in range(2):
+            runs = []
+            for u in range(s * (KEYS // unit), (s + 1) * (KEYS // unit)):
+                t, i = divmod(u, CAPC)
+                if i < first:
+                    at = (t * first + i) * unit
+                    runs.append(before_ref[k, at : at + unit])
+                else:
+                    at = (t * (CAPC - first) + i - first) * unit
+                    runs.append(last[k][at : at + unit])
+            key_value.append(jnp.concatenate(runs, axis=0))
+        keys, values = key_value
+        query = query_ref[s]
+        for h in range(query_ref.shape[2] // HD):
+            cols = slice(h * HD, (h + 1) * HD)
+            scores = lax.dot_general(
+                query[:, cols],
+                keys[:, cols],
+                (((1,), (1,)), ((), ())),
+                preferred_element_type=jnp.float32,
+            ) * (1.0 / math.sqrt(HD))
+            peak = jnp.max(scores, axis=-1, keepdims=True)
+            expo = jnp.exp(scores - peak)
+            weights = (expo / jnp.sum(expo, axis=-1, keepdims=True)).astype(jnp.bfloat16)
+            result = jnp.dot(weights, values[:, cols], preferred_element_type=jnp.float32)
+            result = result.astype(jnp.bfloat16)
+            for c, o_ref in enumerate(out_refs):
+                o_ref[s, :, cols] = result[c * part_rows : (c + 1) * part_rows]
 
 
-def attend(query_blocks, key_values):
-    slots, span, width = query_blocks.shape
+def attend(rows, kv_weight, before, queries, unit, first):
+    peers, span, width = queries.shape
+    depth = rows.shape[1]
     step = math.gcd(HEADS_STEP * HD, width)
-    steps = width // step
+    part = (peers, span // PARTS, step)
+    spec = dict(
+        grid=(width // step,),
+        in_specs=[
+            pl.BlockSpec(rows.shape, lambda h: (0, 0)),
+            pl.BlockSpec((2, depth, step), lambda h: (0, 0, h)),
+            pl.BlockSpec((2, before.shape[1], step), lambda h: (0, 0, h)),
+            pl.BlockSpec((peers, span, step), lambda h: (0, 0, h)),
+        ],
+        out_specs=[pl.BlockSpec(part, lambda h: (0, 0, h))] * PARTS,
+    )
+    made = jax.ShapeDtypeStruct((peers, span // PARTS, width), jnp.bfloat16)
     return pl.pallas_call(
-        attend_kernel,
-        grid=(slots, steps),
-        in_specs=[
-            pl.BlockSpec((1, span, step), lambda s, h: (s, 0, h)),
-            pl.BlockSpec((KEYS, step), lambda s, h: (s, h)),
-            pl.BlockSpec((KEYS, step), lambda s, h: (s, h + steps)),
-        ],
-        out_specs=pl.BlockSpec((1, span, step), lambda s, h: (s, 0, h)),
-        out_shape=jax.ShapeDtypeStruct(query_blocks.shape, jnp.bfloat16),
+        functools.partial(attend_kernel, unit, first),
+        **spec,
+        out_shape=[made] * PARTS,
+        compiler_params=pltpu.CompilerParams(vmem_limit_bytes=52 * 2**20),
         cost_estimate=pl.CostEstimate(
-            flops=4 * slots * span * KEYS * width,
-            bytes_accessed=4 * slots * (span + KEYS) * width,
-            transcendentals=slots * span * KEYS * (width // HD),
+            flops=4 * rows.shape[0] * depth * width + 4 * CAPC * span * KEYS * width,
+            bytes_accessed=4 * depth * width + 2 * rows.size + 2 * before.size,
+            transcendentals=CAPC * span * KEYS * (width // HD),
         ),
-    )(query_blocks, key_values, key_values)
+    )(rows, kv_weight, before, queries)
 
 
 def pick(array, index, count):
@@ -103,28 +134,21 @@
     query_rows = query_rows.transpose(0, 2, 1, 3, 4).reshape(CH_DEV, SPAN, width)
     sent = pick(query_rows, ask, groups * PEER)
     got = lax.all_to_all(sent, OUTER, split_axis=0, concat_axis=0, tiled=True)
-    query_blocks = pick(got, asked, CAPC)
 
-    pieces = CAPC
-    unit = neighbours.shape[0] // pieces
-    key_values = jnp.zeros((tensors, pieces, unit, 2 * width), jnp.bfloat16)
-    for i in range(pieces):
-        block = lax.all_gather(
-            neighbours[i * unit : (i + 1) * unit], "tensor", axis=0, tiled=True
-        )
-        part = jnp.einsum("rd,kde->rke", block, kv_weight, preferred_element_type=jnp.float32)
-        part = part.astype(jnp.bfloat16).reshape(tensors, 1, unit, 2 * width)
-        key_values = lax.dynamic_update_slice(key_values, part, (0, i, 0, 0))
-    key_values = key_values.reshape(CAPC * KEYS, 2 * width)
-
-    attended = attend(query_blocks, key_values)
+    unit = neighbours.shape[0] // CAPC
+    block = lax.all_gather(neighbours[: FIRST * unit], "tensor", axis=0, tiled=True)
+    rest = lax.all_gather(neighbours[FIRST * unit :], "tensor", axis=0, tiled=True)
+    before = jnp.einsum("rd,kde->kre", block, kv_weight, preferred_element_type=jnp.float32)
+    before = before.astype(jnp.bfloat16)
+    attended = attend(
+        rest, kv_weight, before, pick(got, asked, CAPC), unit, FIRST
+    )
 
     outs = []
     part_rows = SPAN // PARTS
     for c in range(PARTS):
-        piece = attended[:, c * part_rows : (c + 1) * part_rows]
         back = lax.all_to_all(
-            pick(piece, answer, groups * PEER), OUTER, split_axis=0, concat_axis=0, tiled=True
+            pick(attended[c], answer, groups * PEER), OUTER, split_axis=0, concat_axis=0, tiled=True
         )
         mine = pick(back, answered, CH_DEV).reshape(CH_DEV * part_rows, width)
         total = jnp.dot(mine, out_weight, preferred_element_type=jnp.float32)

time: 689 us -> 599 us (0.87); the launches traced: 677 us -> 597 us
  local copies, waits for them, and re-layouts: 114 us -> 49.1 us
  matrix products: 168 us -> 110 us
  waiting for transfers between devices: 231 us -> 257 us
  Pallas kernels: 30.6 us -> 47.6 us
    dot_general x5 -> x1, matrix products: 138 us -> 80.3 us  [on_device(): jnp.einsum('rd,kde->kre', block, kv_weight, preferred_element_type=jnp.fl...]
    all_gather x5 -> x2, waiting for transfers between devices: 154 us -> 183 us  [the longest x1 183 us: on_device(): lax.all_gather(neighbours[:FIRST * unit], 'tensor', axis=0, tiled=True)]
    reshape x5 -> x0, local copies, waits for them, and re-layouts: 21.3 us -> none  [on_device(): part = part.astype(jnp.bfloat16).reshape(tensors, 1, unit, 2 * width)]
    dynamic_update_slice x6 -> x0, local copies, waits for them, and re-layouts: 20.8 us -> none  [on_device(): key_values = lax.dynamic_update_slice(key_values, part, (0, i, 0, 0))]
    convert_element_type x5 -> x0, local copies, waits for them, and re-layouts: 17.5 us -> none  [on_device(): part = part.astype(jnp.bfloat16).reshape(tensors, 1, unit, 2 * width)]
    pallas_call x1, Pallas kernels: 30.6 us -> 47.6 us  [attend(): pl.pallas_call(functools.partial(attend_kernel, unit, first), **spec, out...]
    unnamed x69 -> x63, local copies, waits for them, and re-layouts: 40.1 us -> 35.2 us
  transfers between devices with their start and end apart: 9 -> 6, of which waited for: 7 -> 5; matrix products, arithmetic and copies ran while one was open for 28% -> 21% of each run, Pallas kernels for 0% -> 0%
where the time goes in v2:
time: 599 us; the launch traced here: 597 us
  waiting for transfers between devices  257 us (43%)
  matrix products  110 us (18%)
  between operations  91.9 us (15%)
  local copies, waits for them, and re-layouts  49.1 us (8%)
  Pallas kernels  47.6 us (8%)
  blocking collectives  29.8 us (5%)
  starting transfers between devices  9.15 us (2%)
    all_gather x1, waiting for transfers between devices, on_device(): lax.all_gather(neighbours[:FIRST * unit], 'tensor', axis=0, tiled=True)  183 us
    dot_general x1, matrix products, on_device(): jnp.einsum('rd,kde->kre', block, kv_weight, preferred_element_type=jnp.fl...  80.3 us
    reduce_scatter x2, waiting for transfers between devices, on_device(): lax.psum_scatter(total.astype(jnp.bfloat16), 'tensor', scatter_dimension=...  57 us
    pallas_call x1, Pallas kernels, attend(): pl.pallas_call(functools.partial(attend_kernel, unit, first), **spec, out...  47.6 us
    unnamed x63, local copies, waits for them, and re-layouts  35.2 us
    dot_general x2, matrix products, on_device(): total = jnp.dot(mine, out_weight, preferred_element_type=jnp.float32)  30.1 us
    all_to_all x1, blocking collectives, on_device(): lax.all_to_all(pick(attended[c], answer, groups * PEER), OUTER, split_axi...  29.8 us
    all_to_all x1, waiting for transfers between devices, on_device(): lax.all_to_all(pick(attended[c], answer, groups * PEER), OUTER, split_axi...  16.7 us
  transfers between devices with their start and end apart: 6, of which 5 were waited for; matrix products, arithmetic and copies ran while one was open for 21% of the time, Pallas kernels for 0%

profile of v2, /device:TPU:0, one launch (start us, length us, event | category | flops | bytes accessed | tf_op | source)
XLA Modules:
  0.0 597.0 jit_solution(8696218041525921371)
XLA Ops:
  6.5 4.6 slice.154
  43.1 0.7 dynamic-slice_dynamic-update-slice_fusion.20
  43.9 0.7 dynamic-slice_dynamic-update-slice_fusion.19
  44.6 0.7 dynamic-slice_dynamic-update-slice_fusion.18
  48.9 0.7 dynamic-slice_dynamic-update-slice_fusion.12
  54.7 5.2 all-to-all-start
  59.9 2.3 slice.153
  112.9 1.0 dynamic-slice_dynamic-update-slice_fusion.4
  113.9 1.0 dynamic-slice_dynamic-update-slice_fusion.3
  114.9 1.0 dynamic-slice_dynamic-update-slice_fusion.2
  115.9 1.0 dynamic-slice_dynamic-update-slice_fusion.1
  116.9 1.0 dynamic-slice_dynamic-update-slice_fusion.query_ref
  117.8 182.9 %all-gather.5.cloned.1.call-done = bf16[1024,8192]{1,0:T(8,128)(2,1)} async-done(((bf16[256,8192]{1,0:T(8,128)(2,1)}), bf16[1024,8192]{1,0:T(8,128)(2,1)}) %all-gather.5.cloned.1.call-update) | async-done | bytes 16777232 | tf_op jit(solution)/shard_map/all_gather | solution.py:139
  300.8 80.3 %convert_bitcast_fusion.before_ref = bf16[2,1024,2048]{2,1,0:T(8,128)(2,1)} fusion(bf16[2,8192,2048]{2,1,0:T(8,128)(2,1)} %weight_ref.1, bf16[1024,8192]{1,0:T(8,128)(2,1)} %all-gather.5.cloned.1.call-done), kind=kOutput, calls=%fused_computation.4 | convolution fusion | flops 68723671040 | bytes 92274688 | tf_op jit(solution)/shard_map/rd,kde->kre/dot_general | solution.py:141
  381.3 47.6 %shard_map.55 = (bf16[5,32,2048]{2,1,0:T(8,128)(2,1)S(1)}, bf16[5,32,2048]{2,1,0:T(8,128)(2,1)S(1)}) custom-call(bf16[256,8192]{1,0:T(8,128)(2,1)} %all-gather.3.cloned.1.call-done.rows_ref, bf16[2,8192,2048]{2,1,0:T(8,128)(2,1)} %weight_ref.1, bf16[2,1024,2048]{2,1,0:T(8,128)(2,1)} %convert_bitcast_fusion.before_ref, bf16[5,64,2048]{2,1,0:T(8,128)(2,1)} %copy-done), custom_call_target="tpu_custom_call" | custom-call | flops 17850957824 | bytes 79691776 | tf_op jit(solution)/shard_map/pallas_call | solution.py:78
  439.5 3.7 all-to-all-start.1
  452.6 16.7 %all-to-all-done.1 = bf16[16,32,2048]{2,1,0:T(8,128)(2,1)S(1)} async-done(((bf16[16,32,2048]{2,1,0:T(8,128)(2,1)}), bf16[16,32,2048]{2,1,0:T(8,128)(2,1)S(1)}, u32[]{:S(2)}, u32[]{:S(2)}) %all-to-all-start.1) | async-done | bytes 2097184 | tf_op jit(solution)/shard_map/all_to_all | solution.py:150
  469.4 15.0 %convolution_convert_fusion.1 = bf16[160,8192]{1,0:T(8,128)(2,1)} fusion(bf16[160,2048]{1,0:T(8,128)(2,1)S(1)} %bitcast.83, bf16[2048,8192]{1,0:T(8,128)(2,1)} %param.8), kind=kOutput, calls=%fused_computation.3 | convolution fusion | flops 5370019840 | bytes 36831232 | tf_op jit(solution)/shard_map/dot_general | solution.py:154
  485.8 29.8 %all_to_all.15 = bf16[16,32,2048]{2,1,0:T(8,128)(2,1)S(1)} all-to-all(bf16[16,32,2048]{2,1,0:T(8,128)(2,1)} %constant_dynamic-update-slice_fusion.21), channel_id=1, replica_groups=mesh['section'=2,'seq'=4,'tensor'=4] {'section','seq'}, dimensions={0} | all-to-all | bytes 4194304 | tf_op jit(solution)/shard_map/all_to_all | solution.py:150
  515.7 15.1 %convolution_convert_fusion = bf16[160,8192]{1,0:T(8,128)(2,1)} fusion(bf16[160,2048]{1,0:T(8,128)(2,1)S(1)} %bitcast.82, bf16[2048,8192]{1,0:T(8,128)(2,1)} %param.8), kind=kOutput, calls=%fused_computation.2 | convolution fusion | flops 5370019840 | bytes 36831232 | tf_op jit(solution)/shard_map/dot_general | solution.py:154
  530.9 3.0 reduce-scatter.3.cloned.1.call-done
  533.9 54.0 %reduce-scatter.5.cloned.1.call-done = bf16[40,8192]{1,0:T(8,128)(2,1)} async-done(((bf16[160,8192]{1,0:T(8,128)(2,1)}), bf16[40,8192]{1,0:T(8,128)(2,1)}) %reduce-scatter.5.cloned.1.call-update) | async-done | bytes 655376 | tf_op jit(solution)/shard_map/reduce_scatter | solution.py:156
  587.9 1.4 pad_maximum_fusion
  589.3 1.2 copy.13
  (84 shorter events, 34.6 us)
Async XLA Ops:
  6.5 294.2 %all-gather.5.cloned.1.call-start = ((), (), s32[]{:S(2)}) async-start(), calls=%async_computation.6 | async-start | bytes 20971520 | tf_op jit(solution)/shard_map/all_gather | solution.py:139
  11.1 0.7 copy-start.2
  11.1 21.8 %copy-start.1 = (bf16[320,2048]{1,0:T(8,128)(2,1)S(1)}, bf16[320,2048]{1,0:T(8,128)(2,1)}, u32[]{:S(2)}) copy-start(bf16[320,2048]{1,0:T(8,128)(2,1)} %param.5) | copy-start | bytes 3932164
  54.7 58.3 %all-to-all-start = ((bf16[16,64,2048]{2,1,0:T(8,128)(2,1)}), bf16[16,64,2048]{2,1,0:T(8,128)(2,1)}, u32[]{:S(2)}, u32[]{:S(2)}) async-start(bf16[16,64,2048]{2,1,0:T(8,128)(2,1)} %dynamic-slice_dynamic-update-slice_fusion.5), calls=%async_computation | async-start | bytes 8388608 | tf_op jit(solution)/shard_map/all_to_all | solution.py:136
  59.8 321.5 %all-gather.3.cloned.1.call-start = ((), (), s32[]{:S(2)}) async-start(), calls=%async_computation.5 | async-start | bytes 5242880 | tf_op jit(solution)/shard_map/all_gather | solution.py:140
  117.8 263.3 %copy-start = (bf16[5,64,2048]{2,1,0:T(8,128)(2,1)}, bf16[5,64,2048]{2,1,0:T(8,128)(2,1)S(1)}, u32[]{:S(2)}) copy-start(bf16[5,64,2048]{2,1,0:T(8,128)(2,1)S(1)} %dynamic-slice_dynamic-update-slice_fusion.query_ref) | copy-start | bytes 3932164
  439.5 29.8 %all-to-all-start.1 = ((bf16[16,32,2048]{2,1,0:T(8,128)(2,1)}), bf16[16,32,2048]{2,1,0:T(8,128)(2,1)S(1)}, u32[]{:S(2)}, u32[]{:S(2)}) async-start(bf16[16,32,2048]{2,1,0:T(8,128)(2,1)} %constant_dynamic-update-slice_fusion), calls=%async_computation.1 | async-start | bytes 4194304 | tf_op jit(solution)/shard_map/all_to_all | solution.py:150
  443.2 90.8 %reduce-scatter.3.cloned.1.call-start = ((), (), s32[]{:S(2)}) async-start(), calls=%async_computation.7 | async-start | bytes 3276800 | tf_op jit(solution)/shard_map/reduce_scatter | solution.py:156
  484.5 103.5 %reduce-scatter.5.cloned.1.call-start = ((), (), s32[]{:S(2)}) async-start(), calls=%async_computation.8 | async-start | bytes 3276800 | tf_op jit(solution)/shard_map/reduce_scatter | solution.py:156
Sparse Core Ops, SparseCore 0:
  11.3 289.4 all-gather.4
  302.3 78.9 all-gather.2
  484.6 49.2 reduce-scatter.2
  536.1 51.7 reduce-scatter.4
